TPU v7x, 512 devices: a whole 4x4x16 slice. The times are simulated.
512 devices in a mesh: freq: 8 (over x, core), tile: 64 (over z, y).
Axes of the slice: x: 4, y: 4, z: 16, core: 2. Of those that a mesh axis runs over, the one named last changes fastest.
Arguments:
- left_basis: bfloat16 [16, 8192, 2, 1536], P('freq', 'tile'), may hold values from -0.078125 to 0.078125
- right_basis: bfloat16 [16, 8192, 2, 1536], P('freq', 'tile'), may hold values from -0.25 to 0.25
- start_model: float32 [16, 8192, 128], P('freq', 'tile'), may hold values from -3 to 3
- recorded: float32 [16, 8192, 128], P('freq', 'tile'), may hold values from -6 to 6
- tile_ranks: int32 [16, 16], replicated, may hold values from 16 to 96, as said below
- mute_start: int32 [8192, 64], P('tile'), may hold values from 0 to 127
- thresholds: float32 [64], replicated, may hold values from 0.05 to 0.5
Outputs:
- estimate: float32 [16, 8192, 128], P('freq', 'tile')
- misfit: float32 [16, 8192, 128], P('freq', 'tile')
Inputs may be any that keep to these rules, and one draw needn't show every extreme that they name: `tile_ranks`: some tile has rank 96 and some rank 16.
All inputs are finite; a program needn't handle non-finite values.
Results may differ from a plain program's by a relative error of at most 0.013.
Values may be sent and summed in bfloat16 or wider, within the bound.
A program may use at most 64 MiB of HBM per device.

v0:
```python
import math
import jax
import jax.numpy as jnp
from jax import lax
from jax.sharding import PartitionSpec as P

NT = 256
OUTER = 2
STEP_SIZE = 0.5


def phase_table(freq_count):
    sample_index = lax.iota(jnp.int32, NT)[:, None]
    bin_index = lax.iota(jnp.int32, freq_count)[None, :] + NT // 4
    phases = (sample_index * bin_index % NT).astype(jnp.float32) * (2.0 * math.pi / NT)
    return jnp.stack([jnp.cos(phases), -jnp.sin(phases)])


def partials(basis, vector, rank_mask):
    frames = basis.shape[0]
    sources = vector.shape[2] // 2
    inside, rank_slots = rank_mask.shape
    product = jnp.einsum("fnak,fnc->fakc", basis, vector, preferred_element_type=jnp.float32)
    real_part = product[:, 0, :, :sources] + product[:, 1, :, sources:]
    imag_part = product[:, 0, :, sources:] - product[:, 1, :, :sources]
    partial_value = jnp.concatenate([real_part, imag_part], 2).reshape(
        frames, inside, rank_slots, 2 * sources
    )
    partial_value = partial_value * rank_mask[None, :, :, None]
    return partial_value.astype(jnp.bfloat16)


def expand(basis, coefficient):
    frames, height, planes, columns = basis.shape
    inside, share_count, rank_slots, narrow = coefficient.shape[1:]
    blocks = basis.reshape(frames, height, planes, inside, rank_slots)
    product = jnp.einsum(
        "fnajk,fjqkw->fnaqw", blocks, coefficient, preferred_element_type=jnp.float32
    )
    product = product.reshape(frames, height, planes, share_count * narrow)
    sources = share_count * narrow // 2
    real_part = product[:, :, 0, :sources] - product[:, :, 1, sources:]
    imag_part = product[:, :, 0, sources:] + product[:, :, 1, :sources]
    return jnp.concatenate([real_part, imag_part], 2)


def shuffle(partial_value):
    frames, inside, rank_slots, columns = partial_value.shape
    tile_count = lax.axis_size("tile")
    group_size = tile_count // inside
    outgoing = jnp.broadcast_to(
        partial_value[:, :, None], (frames, inside, group_size, rank_slots, columns)
    )
    outgoing = outgoing.reshape(frames, tile_count, rank_slots, columns)
    incoming = lax.all_to_all(outgoing, "tile", split_axis=1, concat_axis=1, tiled=True)
    incoming = incoming.reshape(frames, inside, group_size, rank_slots, columns).astype(jnp.float32)
    return jnp.sum(incoming, 2).astype(jnp.bfloat16)[:, :, None]


def sparsify(estimate, mute_start, thresholds):
    spread = lax.all_to_all(
        estimate.astype(jnp.bfloat16), "freq", split_axis=1, concat_axis=0, tiled=True
    ).astype(estimate.dtype)
    freq_count, rows_here, columns = spread.shape
    sources = columns // 2
    wave_table = phase_table(freq_count)
    stacked = spread.reshape(freq_count, rows_here, 2, sources)
    series = jnp.einsum(
        "atk,knas->nst", wave_table, stacked, precision=lax.Precision.HIGHEST
    ) / math.sqrt(freq_count)
    window = lax.dynamic_slice_in_dim(mute_start, lax.axis_index("freq") * rows_here, rows_here, 0)
    sample_index = lax.iota(jnp.int32, NT)
    series = jnp.where(
        sample_index[None, None, :] >= window[:, :, None], series, jnp.zeros_like(series)
    )
    cutoff = thresholds[None, :, None]
    series = series - jnp.clip(series, -cutoff, cutoff)
    returned = jnp.einsum("nst,atk->knas", series, wave_table, precision=lax.Precision.HIGHEST) * (
        2.0 * math.sqrt(freq_count) / NT
    )
    returned = returned.reshape(freq_count, rows_here, columns)
    return lax.all_to_all(
        returned.astype(jnp.bfloat16), "freq", split_axis=0, concat_axis=1, tiled=True
    ).astype(returned.dtype)


def body(left_basis, right_basis, start_model, recorded, tile_ranks, mute_start, thresholds):
    tile_count = lax.axis_size("tile")
    inside = tile_ranks.shape[0]
    group_size = tile_count // inside
    tile_block = lax.axis_index("tile") // group_size
    levels = lax.iota(jnp.int32, left_basis.shape[3] // inside)
    column_ranks = lax.dynamic_slice_in_dim(tile_ranks, tile_block, 1, 1)
    row_ranks = lax.dynamic_slice_in_dim(tile_ranks, tile_block, 1, 0).reshape(inside, 1)
    right_mask = (levels[None, :] < column_ranks).astype(jnp.float32)
    left_mask = (levels[None, :] < row_ranks).astype(jnp.float32)
    model = start_model
    misfit = recorded
    for outer_step in range(OUTER):
        forward = shuffle(partials(right_basis, model.astype(jnp.bfloat16), right_mask))
        misfit = expand(left_basis, forward) - recorded
        adjoint = shuffle(partials(left_basis, misfit.astype(jnp.bfloat16), left_mask))
        model = model - STEP_SIZE * expand(right_basis, adjoint)
        model = sparsify(model, mute_start, thresholds)
    return (model, misfit)


def solution(mesh):
    return jax.shard_map(
        body,
        mesh=mesh,
        in_specs=(
            P("freq", "tile", None, None),
            P("freq", "tile", None, None),
            P("freq", "tile", None),
            P("freq", "tile", None),
            P(),
            P("tile", None),
            P(),
        ),
        out_specs=(P("freq", "tile", None), P("freq", "tile", None)),
        check_vma=False,
    )
```

profile of v0, /device:TPU:1, one launch (start us, length us, event | category | flops | bytes accessed | tf_op | source)
XLA Modules:
  0.0 716.9 jit_solution(524899450441515643)
XLA Ops:
  0.7 0.9 dynamic-slice_reduce_fusion
  1.7 3.7 copy.151
  5.4 0.6 fusion.49
  6.0 1.4 slice_add_fusion.3
  7.4 1.5 add.105
  8.9 2.5 sub.83
  11.4 2.4 fusion
  13.8 1.7 copy.143
  15.5 2.4 broadcast_in_dim.8
  17.9 19.5 %all-to-all-start = ((bf16[2,64,96,128]{3,2,0,1:T(8,128)(2,1)}), bf16[2,64,96,128]{3,2,0,1:T(8,128)(2,1)}, u32[]{:S(2)}, u32[]{:S(2)}) async-start(bf16[2,64,96,128]{3,2,0,1:T(8,128)(2,1)} %bitcast.221), calls=%async_computation | async-start | bytes 6291456 | tf_op jit(solution)/shard_map/all_to_all | solution.py:55
  37.5 3.7 copy.144
  41.2 1.0 copy.148
  42.2 0.7 fusion.67
  43.0 134.5 %all-to-all-done = bf16[2,64,96,128]{3,2,0,1:T(8,128)(2,1)} async-done(((bf16[2,64,96,128]{3,2,0,1:T(8,128)(2,1)}), bf16[2,64,96,128]{3,2,0,1:T(8,128)(2,1)}, u32[]{:S(2)}, u32[]{:S(2)}) %all-to-all-start) | async-done | bytes 3145760 | tf_op jit(solution)/shard_map/all_to_all | solution.py:55
  177.6 2.4 bitcast_reduce_fusion.3
  180.0 0.5 convolution_bitcast_fusion.8
  180.5 0.6 convolution_bitcast_fusion.2
  181.1 1.4 slice_add_fusion.2
  182.4 2.5 add.110
  184.9 2.5 sub.89
  187.4 2.7 fusion.1
  190.1 2.4 copy.150
  192.5 3.5 broadcast_in_dim.9
  196.1 10.5 %all-to-all-start.1 = ((bf16[2,64,96,128]{3,2,0,1:T(8,128)(2,1)}), bf16[2,64,96,128]{3,2,0,1:T(8,128)(2,1)}, u32[]{:S(2)}, u32[]{:S(2)}) async-start(bf16[2,64,96,128]{3,2,0,1:T(8,128)(2,1)} %bitcast.220), calls=%async_computation.1 | async-start | bytes 6291456 | tf_op jit(solution)/shard_map/all_to_all | solution.py:55
  206.8 138.0 %all-to-all-done.1 = bf16[2,64,96,128]{3,2,0,1:T(8,128)(2,1)} async-done(((bf16[2,64,96,128]{3,2,0,1:T(8,128)(2,1)}), bf16[2,64,96,128]{3,2,0,1:T(8,128)(2,1)}, u32[]{:S(2)}, u32[]{:S(2)}) %all-to-all-start.1) | async-done | bytes 3145760 | tf_op jit(solution)/shard_map/all_to_all | solution.py:55
  344.8 2.4 bitcast_reduce_fusion.2
  347.2 0.5 convolution_bitcast_fusion.7
  347.8 0.8 copy.156
  348.5 12.1 %all-to-all-start.2 = ((bf16[2,128,128]{2,0,1:T(2,128)(2,1)}), bf16[2,128,128]{2,0,1:T(2,128)(2,1)S(1)}, u32[]{:S(2)}, u32[]{:S(2)}) async-start(bf16[2,128,128]{2,0,1:T(2,128)(2,1)} %copy.156), calls=%async_computation.2 | async-start | bytes 131072 | tf_op jit(solution)/shard_map/all_to_all | solution.py:61
  360.7 0.7 neg.17
  361.4 4.0 all-to-all-done.2
  365.6 0.6 fusion.5
  366.2 2.2 fusion.11
  368.7 8.0 %all_to_all.77 = bf16[16,16,128]{2,1,0:T(8,128)(2,1)S(1)} all-to-all(bf16[16,16,128]{2,1,0:T(8,128)(2,1)S(1)} %convert_element_type.128), channel_id=1, replica_groups=mesh['freq'=8,'tile'=64] {'freq'}, dimensions={0} | all-to-all | bytes 131072 | tf_op jit(solution)/shard_map/all_to_all | solution.py:82
  376.7 0.6 convolution_bitcast_fusion.1
  377.4 1.1 slice_add_fusion.1
  378.5 1.5 add.114
  380.0 1.3 sub.95
  381.3 2.4 fusion.2
  383.7 1.7 copy.165
  385.4 0.8 broadcast_in_dim.10
  386.3 146.4 %all_to_all.78 = bf16[2,64,96,128]{3,2,0,1:T(8,128)(2,1)S(1)} all-to-all(bf16[2,64,96,128]{3,2,0,1:T(8,128)(2,1)S(1)} %bitcast.223), channel_id=1, replica_groups=mesh['freq'=8,'tile'=64] {'tile'}, dimensions={1} | all-to-all | bytes 6291456 | tf_op jit(solution)/shard_map/all_to_all | solution.py:55
  532.7 0.5 bitcast_reduce_fusion.1
  533.3 0.5 convolution_bitcast_fusion.6
  533.8 0.4 copy-done.4
  534.2 0.6 convolution_bitcast_fusion
  534.9 0.3 add.118
  535.3 0.4 sub.100
  535.9 0.9 copy.171
  536.7 2.4 broadcast_in_dim.11
  539.1 9.5 %all-to-all-start.5 = ((bf16[2,64,96,128]{3,2,0,1:T(8,128)(2,1)}), bf16[2,64,96,128]{3,2,0,1:T(8,128)(2,1)S(1)}, u32[]{:S(2)}, u32[]{:S(2)}) async-start(bf16[2,64,96,128]{3,2,0,1:T(8,128)(2,1)} %bitcast.222), calls=%async_computation.5 | async-start | bytes 6291456 | tf_op jit(solution)/shard_map/all_to_all | solution.py:55
  548.6 4.9 copy.206
  553.7 133.8 %all-to-all-done.5 = bf16[2,64,96,128]{3,2,0,1:T(8,128)(2,1)S(1)} async-done(((bf16[2,64,96,128]{3,2,0,1:T(8,128)(2,1)}), bf16[2,64,96,128]{3,2,0,1:T(8,128)(2,1)S(1)}, u32[]{:S(2)}, u32[]{:S(2)}) %all-to-all-start.5) | async-done | bytes 3145760 | tf_op jit(solution)/shard_map/all_to_all | solution.py:55
  687.5 0.5 bitcast_reduce_fusion
  688.0 0.9 copy-done.2
  688.9 0.4 convolution_bitcast_fusion.5
  689.6 14.5 %all_to_all.79 = bf16[2,128,128]{2,0,1:T(2,128)(2,1)S(1)} all-to-all(bf16[2,128,128]{2,0,1:T(2,128)(2,1)S(1)} %copy.174), channel_id=1, replica_groups=mesh['freq'=8,'tile'=64] {'freq'}, dimensions={1} | all-to-all | bytes 131072 | tf_op jit(solution)/shard_map/all_to_all | solution.py:61
  704.2 0.6 fusion.7
  704.8 1.6 fusion.10
  706.6 0.7 convert_element_type.136
  707.3 4.0 all-to-all-start.7
  711.4 0.8 copy.180
  712.1 4.1 all-to-all-done.7
  716.2 0.7 copy.179
  (52 shorter events, 2.0 us)
Async XLA Ops:
  0.6 360.0 %copy-start = (s32[128,64]{0,1:T(8,128)S(1)}, s32[128,64]{0,1:T(8,128)}, u32[]{:S(2)}) copy-start(s32[128,64]{0,1:T(8,128)} %param.12) | copy-start | bytes 98308
  0.6 4.8 copy-start.5
  1.7 9.7 %copy-start.6 = (f32[16,96]{1,0:T(8,128)}, f32[16,96]{1,0:T(8,128)S(1)}, u32[]{:S(2)}) copy-start(f32[16,96]{1,0:T(8,128)S(1)} %fusion.65) | copy-start | bytes 18436
  17.9 159.6 %all-to-all-start = ((bf16[2,64,96,128]{3,2,0,1:T(8,128)(2,1)}), bf16[2,64,96,128]{3,2,0,1:T(8,128)(2,1)}, u32[]{:S(2)}, u32[]{:S(2)}) async-start(bf16[2,64,96,128]{3,2,0,1:T(8,128)(2,1)} %bitcast.221), calls=%async_computation | async-start | bytes 6291456 | tf_op jit(solution)/shard_map/all_to_all | solution.py:55
  42.2 138.3 %copy-start.3 = (f32[2,128,128]{1,2,0:T(8,128)}, f32[2,128,128]{1,2,0:T(8,128)S(1)}, u32[]{:S(2)}) copy-start(f32[2,128,128]{1,2,0:T(8,128)S(1)} %copy.148) | copy-start | bytes 393220
  196.1 148.7 %all-to-all-start.1 = ((bf16[2,64,96,128]{3,2,0,1:T(8,128)(2,1)}), bf16[2,64,96,128]{3,2,0,1:T(8,128)(2,1)}, u32[]{:S(2)}, u32[]{:S(2)}) async-start(bf16[2,64,96,128]{3,2,0,1:T(8,128)(2,1)} %bitcast.220), calls=%async_computation.1 | async-start | bytes 6291456 | tf_op jit(solution)/shard_map/all_to_all | solution.py:55
  348.5 16.9 %all-to-all-start.2 = ((bf16[2,128,128]{2,0,1:T(2,128)(2,1)}), bf16[2,128,128]{2,0,1:T(2,128)(2,1)S(1)}, u32[]{:S(2)}, u32[]{:S(2)}) async-start(bf16[2,128,128]{2,0,1:T(2,128)(2,1)} %copy.156), calls=%async_computation.2 | async-start | bytes 131072 | tf_op jit(solution)/shard_map/all_to_all | solution.py:61
  361.4 15.9 %copy-start.9 = (f32[64]{0:T(128)}, f32[64]{0:T(128)S(1)}, u32[]{:S(2)}) copy-start(f32[64]{0:T(128)S(1)} %neg.17) | copy-start | bytes 772
  378.5 2.8 copy-start.7
  533.2 0.9 copy-start.4
  539.1 148.4 %all-to-all-start.5 = ((bf16[2,64,96,128]{3,2,0,1:T(8,128)(2,1)}), bf16[2,64,96,128]{3,2,0,1:T(8,128)(2,1)S(1)}, u32[]{:S(2)}, u32[]{:S(2)}) async-start(bf16[2,64,96,128]{3,2,0,1:T(8,128)(2,1)} %bitcast.222), calls=%async_computation.5 | async-start | bytes 6291456 | tf_op jit(solution)/shard_map/all_to_all | solution.py:55
  687.5 1.4 copy-start.2
  688.9 15.9 %copy-start.8 = (f32[64]{0:T(128)S(1)}, f32[64]{0:T(128)}, u32[]{:S(2)}) copy-start(f32[64]{0:T(128)} %param.13) | copy-start | bytes 772
  688.9 15.9 %copy-start.10 = (f32[64]{0:T(128)S(1)}, f32[64]{0:T(128)}, u32[]{:S(2)}) copy-start(f32[64]{0:T(128)} %copy-done.9) | copy-start | bytes 772
  689.5 27.4 %copy-start.1 = (s32[128,64]{0,1:T(8,128)S(1)}, s32[128,64]{0,1:T(8,128)}, u32[]{:S(2)}) copy-start(s32[128,64]{0,1:T(8,128)} %param.12) | copy-start | bytes 98308
  707.3 8.9 %all-to-all-start.7 = ((bf16[16,16,128]{2,1,0:T(8,128)(2,1)}), bf16[16,16,128]{2,1,0:T(8,128)(2,1)S(1)}, u32[]{:S(2)}, u32[]{:S(2)}) async-start(bf16[16,16,128]{2,1,0:T(8,128)(2,1)} %convert_element_type.136), calls=%async_computation.7 | async-start | bytes 131072 | tf_op jit(solution)/shard_map/all_to_all | solution.py:82
where the time goes:
time: 718 us; the launch traced here: 717 us
  waiting for transfers between devices  414 us (58%)
  blocking collectives  169 us (24%)
  starting transfers between devices  55.6 us (8%)
  local copies, waits for them, and re-layouts  48.7 us (7%)
  other arithmetic  18.9 us (3%)
  matrix products  9.25 us (1%)
    all_to_all x3, waiting for transfers between devices, shuffle(): lax.all_to_all(outgoing, 'tile', split_axis=1, concat_axis=1, tiled=True)  406 us
    all_to_all x1, blocking collectives, shuffle(): lax.all_to_all(outgoing, 'tile', split_axis=1, concat_axis=1, tiled=True)  146 us
    all_to_all x3, starting transfers between devices, shuffle(): lax.all_to_all(outgoing, 'tile', split_axis=1, concat_axis=1, tiled=True)  39.5 us
    all_to_all x1, blocking collectives, sparsify(): lax.all_to_all(estimate.astype(jnp.bfloat16), 'freq', split_axis=1, conca...  14.5 us
  transfers between devices with their start and end apart: 5, of which 5 were waited for; matrix products, arithmetic and copies ran while one was open for 2% of the time, Pallas kernels for 0%

commit v1 on v0

--- a/solution.py
+++ b/solution.py
@@ -52,7 +52,10 @@
         partial_value[:, :, None], (frames, inside, group_size, rank_slots, columns)
     )
     outgoing = outgoing.reshape(frames, tile_count, rank_slots, columns)
-    incoming = lax.all_to_all(outgoing, "tile", split_axis=1, concat_axis=1, tiled=True)
+    incoming = jnp.concatenate(
+        lax.all_to_all(jnp.stack(jnp.split(outgoing, lax.axis_size("tile"), axis=1)), "tile", 0, 0),
+        axis=1,
+    )
     incoming = incoming.reshape(frames, inside, group_size, rank_slots, columns).astype(jnp.float32)
     return jnp.sum(incoming, 2).astype(jnp.bfloat16)[:, :, None]
 

time: 718 us -> 842 us (1.17)
  local copies, waits for them, and re-layouts: 48.7 us -> 162 us
    unnamed x27 -> x277, local copies, waits for them, and re-layouts: 10.6 us -> 127 us
  transfers between devices with their start and end apart: 5 -> 5, of which waited for: 5 -> 5; matrix products, arithmetic and copies ran while one was open for 2% -> 1% of each run, Pallas kernels for 0% -> 0%
where the time goes in v1:
time: 842 us; the launch traced here: 840 us
  waiting for transfers between devices  415 us (49%)
  blocking collectives  168 us (20%)
  local copies, waits for them, and re-layouts  162 us (19%)
  starting transfers between devices  55.8 us (7%)
  other arithmetic  24.3 us (3%)
  matrix products  13.1 us (2%)
    all_to_all x3, waiting for transfers between devices, shuffle(): lax.all_to_all(jnp.stack(jnp.split(outgoing, lax.axis_size('tile'), axis=...  407 us
    all_to_all x1, blocking collectives, shuffle(): lax.all_to_all(jnp.stack(jnp.split(outgoing, lax.axis_size('tile'), axis=...  147 us
    unnamed x277, local copies, waits for them, and re-layouts  127 us
    all_to_all x3, starting transfers between devices, shuffle(): lax.all_to_all(jnp.stack(jnp.split(outgoing, lax.axis_size('tile'), axis=...  39.7 us
  transfers between devices with their start and end apart: 5, of which 5 were waited for; matrix products, arithmetic and copies ran while one was open for 1% of the time, Pallas kernels for 0%

profile of v1, /device:TPU:1, one launch (start us, length us, event | category | flops | bytes accessed | tf_op | source)
XLA Modules:
  0.0 840.0 jit_solution(8400216117129333420)
XLA Ops:
  0.7 0.9 dynamic-slice_reduce_fusion
  1.7 3.7 copy.1452
  6.0 1.4 slice_add_fusion.3
  7.4 1.5 add.105
  8.9 2.5 sub.83
  11.4 2.4 fusion
  13.8 1.7 copy.1444
  15.5 0.8 broadcast_in_dim.8
  44.1 0.6 constant_dynamic-update-slice_fusion.18
  44.7 0.6 constant_dynamic-update-slice_fusion.17
  54.7 0.6 constant_dynamic-update-slice_fusion.1
  55.9 19.5 %all-to-all-start = ((bf16[64,2,1,96,128]{4,3,1,2,0:T(8,128)(2,1)}), bf16[64,2,1,96,128]{4,3,1,2,0:T(8,128)(2,1)}, u32[]{:S(2)}, u32[]{:S(2)}) async-start(bf16[64,2,1,96,128]{4,3,1,2,0:T(8,128)(2,1)} %constant_dynamic-update-slice_fusion), calls=%async_computation | async-start | bytes 6291456 | tf_op jit(solution)/shard_map/all_to_all | solution.py:56
  75.4 3.7 copy.1445
  79.2 1.0 copy.1449
  80.2 0.7 fusion.67
  81.0 134.5 %all-to-all-done = bf16[64,2,1,96,128]{4,3,1,2,0:T(8,128)(2,1)} async-done(((bf16[64,2,1,96,128]{4,3,1,2,0:T(8,128)(2,1)}), bf16[64,2,1,96,128]{4,3,1,2,0:T(8,128)(2,1)}, u32[]{:S(2)}, u32[]{:S(2)}) %all-to-all-start) | async-done | bytes 3145760 | tf_op jit(solution)/shard_map/all_to_all | solution.py:56
  215.5 3.6 reduce_sum.48
  219.1 1.6 convolution_bitcast_fusion.8
  221.3 1.4 slice_add_fusion.2
  222.6 2.5 add.110
  225.1 2.5 sub.89
  227.6 2.7 fusion.1
  230.3 2.4 copy.1451
  232.7 1.9 broadcast_in_dim.9
  262.4 0.6 constant_dynamic-update-slice_fusion.82
  263.1 0.6 constant_dynamic-update-slice_fusion.81
  273.0 0.6 constant_dynamic-update-slice_fusion.65
  274.2 10.5 %all-to-all-start.1 = ((bf16[64,2,1,96,128]{4,3,1,2,0:T(8,128)(2,1)}), bf16[64,2,1,96,128]{4,3,1,2,0:T(8,128)(2,1)}, u32[]{:S(2)}, u32[]{:S(2)}) async-start(bf16[64,2,1,96,128]{4,3,1,2,0:T(8,128)(2,1)} %constant_dynamic-update-slice_fusion.64), calls=%async_computation.1 | async-start | bytes 6291456 | tf_op jit(solution)/shard_map/all_to_all | solution.py:56
  285.0 138.0 %all-to-all-done.1 = bf16[64,2,1,96,128]{4,3,1,2,0:T(8,128)(2,1)} async-done(((bf16[64,2,1,96,128]{4,3,1,2,0:T(8,128)(2,1)}), bf16[64,2,1,96,128]{4,3,1,2,0:T(8,128)(2,1)}, u32[]{:S(2)}, u32[]{:S(2)}) %all-to-all-start.1) | async-done | bytes 3145760 | tf_op jit(solution)/shard_map/all_to_all | solution.py:56
  423.0 3.6 reduce_sum.49
  426.6 1.6 convolution_bitcast_fusion.7
  428.2 0.8 copy.1457
  429.0 12.1 %all-to-all-start.2 = ((bf16[2,128,128]{2,0,1:T(2,128)(2,1)}), bf16[2,128,128]{2,0,1:T(2,128)(2,1)S(1)}, u32[]{:S(2)}, u32[]{:S(2)}) async-start(bf16[2,128,128]{2,0,1:T(2,128)(2,1)} %copy.1457), calls=%async_computation.2 | async-start | bytes 131072 | tf_op jit(solution)/shard_map/all_to_all | solution.py:64
  441.2 0.7 neg.17
  441.8 4.0 all-to-all-done.2
  446.0 0.6 fusion.5
  446.6 2.2 fusion.11
  449.1 8.0 all_to_all.77
  457.8 1.1 slice_add_fusion.1
  458.9 1.5 add.114
  460.4 1.3 sub.95
  461.7 2.4 fusion.2
  464.2 1.7 copy.1466
  465.9 0.8 broadcast_in_dim.10
  467.8 146.5 %all_to_all.78 = bf16[64,2,1,96,128]{4,3,1,2,0:T(8,128)(2,1)} all-to-all(bf16[64,2,1,96,128]{4,3,1,2,0:T(8,128)(2,1)S(1)} %constant_dynamic-update-slice_fusion.128), channel_id=1, replica_groups=mesh['freq'=8,'tile'=64] {'tile'}, dimensions={0} | all-to-all | bytes 6291456 | tf_op jit(solution)/shard_map/all_to_all | solution.py:56
  614.3 2.6 reduce_sum.50
  619.1 0.9 copy.1472
  620.0 0.8 broadcast_in_dim.11
  631.9 0.6 constant_dynamic-update-slice_fusion.237
  634.4 0.6 constant_dynamic-update-slice_fusion.233
  648.6 0.6 constant_dynamic-update-slice_fusion.210
  660.4 9.7 %all-to-all-start.5 = ((bf16[64,2,1,96,128]{4,3,1,2,0:T(8,128)(2,1)}), bf16[64,2,1,96,128]{4,3,1,2,0:T(8,128)(2,1)S(1)}, u32[]{:S(2)}, u32[]{:S(2)}) async-start(bf16[64,2,1,96,128]{4,3,1,2,0:T(8,128)(2,1)} %constant_dynamic-update-slice_fusion.192), calls=%async_computation.5 | async-start | bytes 6291456 | tf_op jit(solution)/shard_map/all_to_all | solution.py:56
  670.1 4.9 copy.1507
  675.1 134.8 %all-to-all-done.5 = bf16[64,2,1,96,128]{4,3,1,2,0:T(8,128)(2,1)S(1)} async-done(((bf16[64,2,1,96,128]{4,3,1,2,0:T(8,128)(2,1)}), bf16[64,2,1,96,128]{4,3,1,2,0:T(8,128)(2,1)S(1)}, u32[]{:S(2)}, u32[]{:S(2)}) %all-to-all-start.5) | async-done | bytes 3145760 | tf_op jit(solution)/shard_map/all_to_all | solution.py:56
  810.0 1.7 reduce_sum.51
  811.6 2.1 convolution_bitcast_fusion.5
  813.9 13.3 %all_to_all.79 = bf16[2,128,128]{2,0,1:T(2,128)(2,1)S(1)} all-to-all(bf16[2,128,128]{2,0,1:T(2,128)(2,1)S(1)} %copy.1475), channel_id=1, replica_groups=mesh['freq'=8,'tile'=64] {'freq'}, dimensions={1} | all-to-all | bytes 131072 | tf_op jit(solution)/shard_map/all_to_all | solution.py:64
  827.3 0.6 fusion.7
  828.0 1.6 fusion.10
  829.7 0.7 convert_element_type.136
  830.5 4.0 all-to-all-start.7
  834.5 0.8 copy.1481
  835.3 4.1 all-to-all-done.7
  839.4 0.7 copy.1480
  (306 shorter events, 119.2 us)
Async XLA Ops:
  0.6 440.4 %copy-start = (s32[128,64]{0,1:T(8,128)S(1)}, s32[128,64]{0,1:T(8,128)}, u32[]{:S(2)}) copy-start(s32[128,64]{0,1:T(8,128)} %param.12) | copy-start | bytes 98308
  0.6 4.8 copy-start.4
  1.7 9.7 %copy-start.5 = (f32[16,96]{1,0:T(8,128)}, f32[16,96]{1,0:T(8,128)S(1)}, u32[]{:S(2)}) copy-start(f32[16,96]{1,0:T(8,128)S(1)} %fusion.65) | copy-start | bytes 18436
  55.9 159.6 %all-to-all-start = ((bf16[64,2,1,96,128]{4,3,1,2,0:T(8,128)(2,1)}), bf16[64,2,1,96,128]{4,3,1,2,0:T(8,128)(2,1)}, u32[]{:S(2)}, u32[]{:S(2)}) async-start(bf16[64,2,1,96,128]{4,3,1,2,0:T(8,128)(2,1)} %constant_dynamic-update-slice_fusion), calls=%async_computation | async-start | bytes 6291456 | tf_op jit(solution)/shard_map/all_to_all | solution.py:56
  80.2 140.5 %copy-start.2 = (f32[2,128,128]{1,2,0:T(8,128)}, f32[2,128,128]{1,2,0:T(8,128)S(1)}, u32[]{:S(2)}) copy-start(f32[2,128,128]{1,2,0:T(8,128)S(1)} %copy.1449) | copy-start | bytes 393220
  274.2 148.7 %all-to-all-start.1 = ((bf16[64,2,1,96,128]{4,3,1,2,0:T(8,128)(2,1)}), bf16[64,2,1,96,128]{4,3,1,2,0:T(8,128)(2,1)}, u32[]{:S(2)}, u32[]{:S(2)}) async-start(bf16[64,2,1,96,128]{4,3,1,2,0:T(8,128)(2,1)} %constant_dynamic-update-slice_fusion.64), calls=%async_computation.1 | async-start | bytes 6291456 | tf_op jit(solution)/shard_map/all_to_all | solution.py:56
  429.0 16.9 %all-to-all-start.2 = ((bf16[2,128,128]{2,0,1:T(2,128)(2,1)}), bf16[2,128,128]{2,0,1:T(2,128)(2,1)S(1)}, u32[]{:S(2)}, u32[]{:S(2)}) async-start(bf16[2,128,128]{2,0,1:T(2,128)(2,1)} %copy.1457), calls=%async_computation.2 | async-start | bytes 131072 | tf_op jit(solution)/shard_map/all_to_all | solution.py:64
  441.8 15.3 %copy-start.8 = (f32[64]{0:T(128)}, f32[64]{0:T(128)S(1)}, u32[]{:S(2)}) copy-start(f32[64]{0:T(128)S(1)} %neg.17) | copy-start | bytes 772
  457.8 3.9 copy-start.6
  614.3 3.0 copy-start.3
  660.4 149.6 %all-to-all-start.5 = ((bf16[64,2,1,96,128]{4,3,1,2,0:T(8,128)(2,1)}), bf16[64,2,1,96,128]{4,3,1,2,0:T(8,128)(2,1)S(1)}, u32[]{:S(2)}, u32[]{:S(2)}) async-start(bf16[64,2,1,96,128]{4,3,1,2,0:T(8,128)(2,1)} %constant_dynamic-update-slice_fusion.192), calls=%async_computation.5 | async-start | bytes 6291456 | tf_op jit(solution)/shard_map/all_to_all | solution.py:56
  811.6 16.4 %copy-start.7 = (f32[64]{0:T(128)S(1)}, f32[64]{0:T(128)}, u32[]{:S(2)}) copy-start(f32[64]{0:T(128)} %param.13) | copy-start | bytes 772
  811.6 16.4 %copy-start.9 = (f32[64]{0:T(128)S(1)}, f32[64]{0:T(128)}, u32[]{:S(2)}) copy-start(f32[64]{0:T(128)} %copy-done.8) | copy-start | bytes 772
  811.6 28.4 %copy-start.1 = (s32[128,64]{0,1:T(8,128)S(1)}, s32[128,64]{0,1:T(8,128)}, u32[]{:S(2)}) copy-start(s32[128,64]{0,1:T(8,128)} %param.12) | copy-start | bytes 98308
  830.5 8.9 %all-to-all-start.7 = ((bf16[16,16,128]{2,1,0:T(8,128)(2,1)}), bf16[16,16,128]{2,1,0:T(8,128)(2,1)S(1)}, u32[]{:S(2)}, u32[]{:S(2)}) async-start(bf16[16,16,128]{2,1,0:T(8,128)(2,1)} %convert_element_type.136), calls=%async_computation.7 | async-start | bytes 131072 | tf_op jit(solution)/shard_map/all_to_all | solution.py:85
